TPU v7x, 32 devices: a whole 2x2x4 slice. The times are simulated.
32 devices in a mesh: groups: 2 (over y), particle: 4 (over z), slab: 2 (over x), rep: 2 (over core).
Axes of the slice: x: 2, y: 2, z: 4, core: 2. Of those that a mesh axis runs over, the one named last changes fastest.
Arguments:
- images: float32 [64, 384, 384], P(('groups', 'particle', 'slab', 'rep')), parts along dimension 0, may hold values from -6 to 6
- poses: int32 [64], P(('groups', 'particle', 'slab', 'rep')), parts along dimension 0, may hold values from 0 to 31
- plane_index: int32 [32, 2, 4, 9], P(None, 'slab'), may hold values from 0 to 2
- plane_weight: float32 [32, 2, 4, 9], P(None, 'slab'), may hold values from 0.05 to 1
- shell_counts: int32 [576], P('groups'), parts along dimension 0, may hold values from 8 to 31
Outputs:
- volume: float32 [16, 384, 384], P(('groups', 'slab'), ('particle', 'rep')), parts along dimension 0
There are 2 independent parts, one for each index of `groups`. A program takes and returns all parts, laid end to end along the dimension named above; an argument that names none is the same for every part. Nothing has to cross between parts.
All inputs are finite; a program needn't handle non-finite values.
Results may differ from a plain program's by a relative error of at most 0.0065.
Values may be sent and summed in bfloat16 or wider, within the bound.
A program may use at most 64 MiB of HBM per device.

v0:
```python
import math

import jax
import jax.numpy as jnp
from jax import lax
from jax.sharding import PartitionSpec as P

ZS = 3
OZS = 4
TSIDE = 3


def phase_table(freq_list, positions, box_size):
    product = freq_list[:, None] * positions[None, :] % box_size
    return 2.0 * math.pi / box_size * product.astype(jnp.float32)


def centered(indices, box_size):
    return jnp.where(indices < box_size // 2, indices, indices - box_size)


def shell_index(squared):
    estimate = jnp.floor(jnp.sqrt(squared.astype(jnp.float32))).astype(jnp.int32)
    estimate = estimate - (estimate * estimate > squared).astype(jnp.int32)
    estimate = estimate + ((estimate + 1) * (estimate + 1) <= squared).astype(jnp.int32)
    return estimate


def grid_weight(positions, box_size):
    return jnp.sinc(centered(positions, box_size).astype(jnp.float32) / box_size) ** 2


def spectra_of(pictures, cos_table, sin_table):
    box_size = cos_table.shape[0]
    cos_sin = jnp.concatenate([cos_table, sin_table], axis=1)
    table_pair = jnp.stack([cos_sin, jnp.concatenate([-sin_table, cos_table], axis=1)])

    def single(picture):
        section_one = jnp.dot(picture, cos_sin, preferred_element_type=jnp.float32)
        real_part = section_one[:, :box_size].astype(jnp.bfloat16)
        imag_part = (-section_one[:, box_size:]).astype(jnp.bfloat16)
        stacked = jnp.concatenate([real_part, imag_part], axis=0)
        return jnp.einsum(
            "aky,yx->akx", table_pair, stacked, preferred_element_type=jnp.float32
        ).astype(jnp.bfloat16)

    return lax.map(single, pictures)


def insert_images(running, spectra, pose_piece, local_index, local_weight):
    highest = lax.Precision.HIGHEST
    pose_total = local_index.shape[0]
    entry_total = local_index.shape[1]
    tile_total = local_index.shape[2]
    plane_total = running.shape[0]
    box_size = spectra.shape[-1]
    tile_size = box_size // TSIDE
    count = pose_piece.shape[0]
    onehot = (pose_piece[:, None] == jnp.arange(pose_total, dtype=jnp.int32)[None, :]).astype(
        jnp.float32
    )
    chosen_index = jnp.dot(
        onehot,
        local_index.reshape(pose_total, entry_total * tile_total).astype(jnp.float32),
        precision=highest,
    )
    chosen_weight = jnp.dot(
        onehot, local_weight.reshape(pose_total, entry_total * tile_total), precision=highest
    )
    chosen_index = chosen_index.reshape(count, entry_total, tile_total)
    chosen_weight = chosen_weight.reshape(count, entry_total, tile_total)
    planes = jnp.arange(plane_total).astype(jnp.float32)
    matches = (chosen_index[..., None] == planes).astype(jnp.float32)
    per_plane = jnp.sum(matches * chosen_weight[..., None], axis=1)
    mixing = (
        per_plane.transpose(2, 1, 0).reshape(plane_total, TSIDE, TSIDE, count).astype(jnp.bfloat16)
    )
    tiled = spectra.reshape(count, 2, TSIDE, tile_size, TSIDE, tile_size)
    added = jnp.einsum("zabi,icaybx->zcaybx", mixing, tiled, preferred_element_type=jnp.float32)
    return added.reshape(plane_total, 2, box_size, box_size)


def body(images, poses, plane_index, plane_weight, shell_counts):
    highest = lax.Precision.HIGHEST
    box_size = images.shape[-1]
    slab_index = lax.axis_index("slab")
    slab_total = lax.axis_size("slab")
    pencil_index = lax.axis_index(("particle", "rep"))
    positions = jnp.arange(box_size, dtype=jnp.int32)
    angles = phase_table(positions, positions, box_size)
    root_box = math.sqrt(box_size)
    cos_table = (jnp.cos(angles) / root_box).astype(jnp.bfloat16)
    sin_table = (jnp.sin(angles) / root_box).astype(jnp.bfloat16)
    local_index = plane_index[:, 0]
    local_weight = plane_weight[:, 0]
    empty_window = jnp.zeros((ZS, 2, box_size, box_size), jnp.float32)
    partial_value = insert_images(
        empty_window,
        spectra_of(
            lax.all_gather(images.astype(jnp.bfloat16), "slab", axis=0, tiled=True),
            cos_table,
            sin_table,
        ),
        lax.all_gather(poses, "slab", axis=0, tiled=True),
        local_index,
        local_weight,
    )
    summed = lax.psum_scatter(partial_value, ("particle", "rep"), scatter_dimension=2, tiled=True)
    row_total = summed.shape[2]
    window_planes = ZS * slab_total
    depth_freq = slab_index * ZS + jnp.arange(ZS, dtype=jnp.int32) - window_planes // 2
    row_freq = centered(pencil_index * row_total + jnp.arange(row_total, dtype=jnp.int32), box_size)
    column_freq = centered(positions, box_size)
    inverse_root = 1.0 / jnp.sqrt(shell_counts.astype(jnp.float32))
    shell_ids = jnp.arange(inverse_root.shape[0], dtype=jnp.int32)

    def plane_scale(depth_value):
        squared = depth_value * depth_value + row_freq[:, None] ** 2 + column_freq[None, :] ** 2
        member = (shell_index(squared)[:, :, None] == shell_ids[None, None, :]).astype(jnp.float32)
        return jnp.dot(member, inverse_root, precision=highest)

    shell_scale = lax.map(plane_scale, depth_freq)
    normed = summed * shell_scale[:, None]
    cosine = jnp.cos(angles) / root_box
    sine = jnp.sin(angles) / root_box
    inverse_table = jnp.stack([jnp.stack([cosine, sine]), jnp.stack([-sine, cosine])])
    across = jnp.einsum("zcyk,cakx->zaxy", normed, inverse_table, precision=highest)
    pencils = lax.all_to_all(across, ("particle", "rep"), split_axis=2, concat_axis=3, tiled=True)
    pencil_lines = jnp.einsum("zcxk,caky->zaxy", pencils, inverse_table, precision=highest)
    column_total = pencil_lines.shape[2]
    out_planes = OZS * slab_total
    spacing = box_size // out_planes
    own_rows = slab_index * OZS + jnp.arange(OZS, dtype=jnp.int32)
    depth_angle = phase_table(
        depth_freq, jnp.arange(lax.axis_size("slab") * OZS, dtype=jnp.int32) * spacing, box_size
    )
    depth_cos = jnp.cos(depth_angle) / math.sqrt(window_planes)
    depth_sin = jnp.sin(depth_angle) / math.sqrt(window_planes)
    raw = lax.psum_scatter(
        jnp.einsum("zo,zxy->oxy", depth_cos, pencil_lines[:, 0], precision=highest)
        - jnp.einsum("zo,zxy->oxy", depth_sin, pencil_lines[:, 1], precision=highest),
        "slab",
        scatter_dimension=0,
        tiled=True,
    )
    column_pos = pencil_index * column_total + jnp.arange(column_total, dtype=jnp.int32)
    correction = (
        grid_weight(own_rows * spacing, box_size)[:, None, None]
        * grid_weight(column_pos, box_size)[None, :, None]
        * grid_weight(positions, box_size)[None, None, :]
    )
    return raw / correction


def solution(mesh):
    in_specs = (
        P(("groups", "particle", "slab", "rep"), None, None),
        P(("groups", "particle", "slab", "rep")),
        P(None, "slab", None, None),
        P(None, "slab", None, None),
        P("groups"),
    )
    out_specs = P(("groups", "slab"), ("particle", "rep"), None)
    return jax.shard_map(body, mesh=mesh, in_specs=in_specs, out_specs=out_specs, check_vma=False)
```

profile of v0, /device:TPU:0, one launch (start us, length us, event | category | flops | bytes accessed | tf_op | source)
XLA Modules:
  0.0 176.3 jit_solution(17946691357532406395)
XLA Ops:
  6.6 2.2 %convert_element_type.160 = bf16[2,384,384]{2,1,0:T(8,128)(2,1)} convert(f32[2,384,384]{2,1,0:T(8,128)} %param.9) | non-fusion elementwise | flops 294912 | bytes 1769472 | tf_op jit(solution)/shard_map/convert_element_type | solution.py:100
  8.9 0.6 dynamic-slice
  10.4 5.2 %all-reduce = s32[4]{0:T(128)S(1)} all-reduce(s32[4]{0:T(128)S(1)} %dynamic-update-slice), channel_id=1, replica_groups=mesh['groups'=2,'particle'=4,'slab'=2,'rep'=2] {'slab'}, use_global_device_ids=true, to_apply=%add | all-reduce | flops 4 | bytes 32
  15.6 0.3 fusion.77
  16.5 2.3 %fusion.49 = bf16[384,384]{1,0:T(8,128)(2,1)S(1)} fusion(), kind=kLoop, calls=%fused_computation.78 | loop fusion | flops 2064384 | bytes 294912 | tf_op jit(solution)/shard_map/neg | solution.py:36
  18.9 2.6 %multiply_convert_fusion = (bf16[384,384]{1,0:T(8,128)(2,1)S(1)}, bf16[384,384]{1,0:T(8,128)(2,1)S(1)}) fusion(), kind=kLoop, calls=%fused_computation.56 | loop fusion | flops 1916928 | bytes 589824 | tf_op jit(solution)/shard_map/convert_element_type | solution.py:93
  21.7 12.8 %all-gather.2.cloned.1.call-done = bf16[4,384,384]{2,1,0:T(8,128)(2,1)} async-done(((bf16[2,384,384]{2,1,0:T(8,128)(2,1)}), bf16[4,384,384]{2,1,0:T(8,128)(2,1)}) %all-gather.2.cloned.1.call-update) | async-done | bytes 1179664 | tf_op jit(solution)/shard_map/all_gather | solution.py:100
  34.5 12.2 %while.24 = (s32[]{:T(128)}, bf16[4,2,384,384]{2,3,1,0:T(8,128)(2,1)}, bf16[4,384,384]{2,1,0:T(8,128)(2,1)}, bf16[384,768]{1,0:T(8,128)(2,1)S(1)}, bf16[2,384,768]{2,1,0:T(8,128)(2,1)S(1)}, /*index=5*/s32[]{:T(128)}) while((s32[]{:T(128)}, bf16[4,2,384,384]{2,3,1,0:T(8,128)(2,1)}, bf16[4,384,384]{2,1,0:T(8,128)(2,1)}, ...), condition=%wide.region_1.2_spmd, body=%wide.region_0.1_spmd.sunk | while | flops 681246720 | bytes 5899333 | solution.py:47
  34.5 1.4 fusion.135
  36.0 1.5 fusion.137
  37.6 1.4 fusion.135
  39.1 1.5 fusion.137
  40.6 1.4 fusion.135
  42.1 1.6 fusion.137
  43.7 1.4 fusion.135
  45.2 1.5 fusion.137
  46.7 5.9 %reshape.382 = bf16[4,2,3,128,3,128]{3,2,5,4,1,0:T(4,128)(2,1)S(1)} reshape(bf16[4,2,384,384]{2,3,1,0:T(8,128)(2,1)} %get-tuple-element.117) | data formatting | bytes 4718592 | tf_op jit(solution)/shard_map/reshape | solution.py:78
  52.6 3.7 %copy.68 = bf16[4,2,3,128,3,128]{5,0,3,1,4,2:T(4,128)(2,1)} copy(bf16[4,2,3,128,3,128]{3,2,5,4,1,0:T(4,128)(2,1)S(1)} %reshape.382) | data formatting | bytes 4718592 | tf_op jit(solution)/shard_map/reshape | solution.py:78
  56.3 3.0 %convolution_bitcast_fusion = f32[3,2,3,128,3,128]{5,0,3,1,4,2:T(4,128)S(1)} fusion(bf16[4,2,3,128,3,128]{5,0,3,1,4,2:T(4,128)(2,1)} %copy.68, bf16[3,3,3,4,1,1]{3,0,5,4,2,1:T(4,128)(2,1)S(1)} %copy.78), kind=kOutput, calls=%fused_computation.38 | convolution fusion | flops 7077888 | bytes 5898456 | tf_op jit(solution)/shard_map/zabi,icaybx->zcaybx/dot_general | solution.py:79
  59.3 4.6 %copy.70 = f32[3,2,3,128,3,128]{5,4,3,2,1,0:T(4,128)} copy(f32[3,2,3,128,3,128]{5,0,3,1,4,2:T(4,128)S(1)} %convolution_bitcast_fusion) | data formatting | bytes 7077888 | tf_op jit(solution)/shard_map/zabi,icaybx->zcaybx/transpose | solution.py:79
  63.9 6.7 %reshape.364 = f32[3,2,384,384]{3,2,1,0:T(8,128)} reshape(f32[3,2,3,128,3,128]{5,4,3,2,1,0:T(4,128)} %copy.70) | data formatting | bytes 7077888 | tf_op jit(solution)/shard_map/reshape | solution.py:80
  70.7 0.6 copy-done.3
  71.3 2.3 %fusion.47 = f32[1,384,384]{2,1,0:T(8,128)S(1)} fusion(), kind=kLoop, calls=%fused_computation.74 | loop fusion | flops 1622016 | bytes 589824 | tf_op jit(solution)/shard_map/neg | solution.py:126
  73.6 2.4 %sine_multiply_fusion = (f32[1,384,384]{2,1,0:T(8,128)S(1)}, f32[1,384,384]{2,1,0:T(8,128)S(1)}) fusion(), kind=kLoop, calls=%fused_computation.61 | loop fusion | flops 1622016 | bytes 1179648 | tf_op jit(solution)/shard_map/div | solution.py:125
  76.2 26.2 %while.25 = (s32[]{:T(128)}, f32[3,48,384]{2,1,0:T(8,128)S(1)}, s32[3]{0:T(128)S(1)}, f32[288]{0:T(512)}, s32[]{:T(128)}, /*index=5*/f32[288,1,1]{0,1,2:T(1,128)S(1)}, s32[]{:T(128)}) while((s32[]{:T(128)}, f32[3,48,384]{2,1,0:T(8,128)S(1)}, s32[3]{0:T(128)S(1)}, f32[288]{0:T(512)}, s32[]{:T(128)}, ...), condition=%wide.wide.region_5.6_spmd.clone, body=%wide.wide.region_4.5_spmd.clone.sunk | while | flops 69250848 | bytes 373361 | solution.py:122
  76.2 0.7 dynamic_slice.19
  78.3 6.6 %fusion.141 = f32[1,48,384]{2,0,1:T(1,128)S(1)} fusion(f32[288,1,1]{0,1,2:T(1,128)S(1)} %get-tuple-element.290, s32[48,384]{1,0:T(8,128)S(1)} %convert_add_fusion.3), kind=kOutput, calls=%fused_computation.18.clone.clone.1 | convolution fusion | flops 69009408 | bytes 148608 | tf_op jit(solution)/shard_map/while/body/eval_jaxpr/dot_general | solution.py:120
  84.9 0.7 dynamic_slice.19
  87.1 6.6 %fusion.141 = f32[1,48,384]{2,0,1:T(1,128)S(1)} fusion(f32[288,1,1]{0,1,2:T(1,128)S(1)} %get-tuple-element.290, s32[48,384]{1,0:T(8,128)S(1)} %convert_add_fusion.3), kind=kOutput, calls=%fused_computation.18.clone.clone.1 | convolution fusion | flops 69009408 | bytes 148608 | tf_op jit(solution)/shard_map/while/body/eval_jaxpr/dot_general | solution.py:120
  93.7 0.7 dynamic_slice.19
  95.8 6.6 %fusion.141 = f32[1,48,384]{2,0,1:T(1,128)S(1)} fusion(f32[288,1,1]{0,1,2:T(1,128)S(1)} %get-tuple-element.290, s32[48,384]{1,0:T(8,128)S(1)} %convert_add_fusion.3), kind=kOutput, calls=%fused_computation.18.clone.clone.1 | convolution fusion | flops 69009408 | bytes 148608 | tf_op jit(solution)/shard_map/while/body/eval_jaxpr/dot_general | solution.py:120
  102.4 12.1 %reduce-scatter.3.cloned.1.call-done = f32[3,2,48,384]{3,2,1,0:T(8,128)} async-done(((f32[3,2,384,384]{3,2,1,0:T(8,128)}), f32[3,2,48,384]{3,2,1,0:T(8,128)}) %reduce-scatter.3.cloned.1.call-update) | async-done | bytes 442384 | tf_op jit(solution)/shard_map/reduce_scatter | solution.py:108
  114.5 3.3 %fusion.30 = f32[3,2,384,48]{2,3,0,1:T(8,128)} fusion(f32[1,2,384,384]{3,2,0,1:T(8,128)S(1)} %get-tuple-element.157, f32[1,2,384,384]{3,2,0,1:T(8,128)S(1)} %get-tuple-element.156, f32[3,2,48,384]{3,2,1,0:T(8,128)} %reduce-scatter.3.cloned.1.call-done, f32[3,48,384]{2,1,0:T(8,128)S(1)} %get-tuple-element.118), kind=kOutput, calls=%fused_computation.42 | convolution fusion | flops 1019916288 | bytes 3465216 | tf_op jit(solution)/shard_map/zcyk,cakx->zaxy/dot_general | solution.py:127
  117.9 2.4 %copy.71 = f32[3,2,384,48]{3,1,0,2:T(2,128)S(1)} copy(f32[3,2,384,48]{2,3,0,1:T(8,128)} %fusion.30) | data formatting | bytes 884736 | tf_op jit(solution)/shard_map/zcyk,cakx->zaxy/transpose | solution.py:127
  120.2 2.8 %reshape.386 = f32[8,1,13824]{2,1,0:T(1,128)} reshape(f32[384,3,2,48]{3,2,1,0:T(2,128)S(1)} %bitcast.117) | data formatting | bytes 884736
  123.1 3.5 %all-to-all-start = ((f32[8,1,13824]{2,1,0:T(1,128)}), f32[8,1,13824]{2,1,0:T(1,128)S(1)}, u32[]{:S(2)}, u32[]{:S(2)}) async-start(f32[8,1,13824]{2,1,0:T(1,128)} %reshape.386), calls=%async_computation.1 | async-start | bytes 884736 | tf_op jit(solution)/shard_map/all_to_all | solution.py:128
  126.8 13.2 %all-to-all-done = f32[8,1,13824]{2,1,0:T(1,128)S(1)} async-done(((f32[8,1,13824]{2,1,0:T(1,128)}), f32[8,1,13824]{2,1,0:T(1,128)S(1)}, u32[]{:S(2)}, u32[]{:S(2)}) %all-to-all-start) | async-done | bytes 442400 | tf_op jit(solution)/shard_map/all_to_all | solution.py:128
  140.1 0.5 broadcast.597
  140.6 2.5 %reduce.2 = f32[8,13824]{1,0:T(8,128)} reduce(f32[8,1,13824]{2,1,0:T(1,128)S(1)} %all-to-all-done, f32[]{:T(128)} %broadcast.597), dimensions={1}, to_apply=%all_to_all.13.reduce_sub_computation | reduce | bytes 884740 | tf_op jit(solution)/shard_map/all_to_all | solution.py:128
  143.1 2.9 %reshape.387 = f32[384,3,2,48]{3,2,1,0:T(2,128)S(1)} reshape(f32[8,13824]{1,0:T(8,128)} %reduce.2) | data formatting | bytes 884736
  146.0 1.7 copy.95
  147.8 1.6 reshape.378
  149.4 1.6 fusion.31
  151.0 0.9 fusion.45
  151.9 0.9 convolution_subtract_fusion
  152.8 0.9 copy.75
  153.9 14.1 %reduce-scatter.5.cloned.1.call-done = f32[4,48,384]{2,1,0:T(8,128)} async-done(((f32[8,48,384]{2,1,0:T(8,128)}), f32[4,48,384]{2,1,0:T(8,128)}) %reduce-scatter.5.cloned.1.call-update) | async-done | bytes 294928 | tf_op jit(solution)/shard_map/reduce_scatter | solution.py:139
  168.0 1.8 %multiply_divide_fusion = f32[4,48,384]{2,1,0:T(8,128)} fusion(f32[4,48,384]{2,1,0:T(8,128)} %reduce-scatter.5.cloned.1.call-done, f32[384]{0:T(512)S(1)} %fusion.57, f32[4,48]{1,0:T(4,128)S(1)} %broadcast_multiply_fusion), kind=kLoop, calls=%fused_computation.73 | loop fusion | flops 147456 | bytes 592128 | tf_op jit(solution)/shard_map/div | solution.py:152
  (67 shorter events, 2.8 us)
Async XLA Ops:
  6.5 2.3 %copy-start.5 = (u32[32]{0:T(128)S(1)}, u32[32]{0:T(128)}, u32[]{:S(2)}) copy-start(u32[32]{0:T(128)} %constant.199) | copy-start | bytes 388
  6.5 3.6 %copy-start.4 = (s32[2]{0:T(128)S(1)}, s32[2]{0:T(128)}, u32[]{:S(2)}) copy-start(s32[2]{0:T(128)} %param.10) | copy-start | bytes 28
  6.5 9.0 %copy-start.1 = (s32[32,1,4,9]{0,2,3,1:T(4,128)S(1)}, s32[32,1,4,9]{0,2,3,1:T(4,128)}, u32[]{:S(2)}) copy-start(s32[32,1,4,9]{0,2,3,1:T(4,128)} %param.11) | copy-start | bytes 13828
  6.5 9.3 %copy-start = (f32[32,1,4,9]{0,2,3,1:T(4,128)S(1)}, f32[32,1,4,9]{0,2,3,1:T(4,128)}, u32[]{:S(2)}) copy-start(f32[32,1,4,9]{0,2,3,1:T(4,128)} %param.12) | copy-start | bytes 13828
  6.5 28.0 %all-gather.2.cloned.1.call-start = ((), (), s32[]{:S(2)}) async-start(), calls=%async_computation.3 | async-start | bytes 1769472 | tf_op jit(solution)/shard_map/all_gather | solution.py:100
  8.8 105.8 %reduce-scatter.3.cloned.1.call-start = ((), (), s32[]{:S(2)}) async-start(), calls=%async_computation.4 | async-start | bytes 3981312 | tf_op jit(solution)/shard_map/reduce_scatter | solution.py:108
  70.6 0.7 copy-start.3
  71.3 4.9 %copy-start.2 = (f32[288]{0:T(512)}, f32[288]{0:T(512)S(1)}, u32[]{:S(2)}) copy-start(f32[288]{0:T(512)S(1)} %convert_rsqrt_fusion) | copy-start | bytes 3460
  123.1 17.0 %all-to-all-start = ((f32[8,1,13824]{2,1,0:T(1,128)}), f32[8,1,13824]{2,1,0:T(1,128)S(1)}, u32[]{:S(2)}, u32[]{:S(2)}) async-start(f32[8,1,13824]{2,1,0:T(1,128)} %reshape.386), calls=%async_computation.1 | async-start | bytes 884736 | tf_op jit(solution)/shard_map/all_to_all | solution.py:128
  126.5 41.4 %reduce-scatter.5.cloned.1.call-start = ((), (), s32[]{:S(2)}) async-start(), calls=%async_computation.5 | async-start | bytes 884736 | tf_op jit(solution)/shard_map/reduce_scatter | solution.py:139
Sparse Core Ops, SparseCore 0:
  8.9 25.5 all-gather.1
  70.8 43.7 reduce-scatter.2
  153.8 14.1 reduce-scatter.4
where the time goes:
time: 177 us; the launch traced here: 176 us
  waiting for transfers between devices  52.3 us (30%)
  matrix products  41.8 us (24%)
  local copies, waits for them, and re-layouts  37.7 us (21%)
  other arithmetic  17.5 us (10%)
  between operations  14 us (8%)
  blocking collectives  5.19 us (3%)
  loops' own time  4.03 us (2%)
  starting transfers between devices  3.8 us (2%)
    dot_general x3, matrix products, plane_scale(): return jnp.dot(member, inverse_root, precision=highest)  19.7 us
    reduce_scatter x1, waiting for transfers between devices, body(): lax.psum_scatter(jnp.einsum('zo,zxy->oxy', depth_cos, pencil_lines[:, 0],...  14.1 us
    all_to_all x1, waiting for transfers between devices, body(): lax.all_to_all(across, ('particle', 'rep'), split_axis=2, concat_axis=3,...  13.2 us
    all_gather x1, waiting for transfers between devices, body(): lax.all_gather(images.astype(jnp.bfloat16), 'slab', axis=0, tiled=True)  12.8 us
    reduce_scatter x1, waiting for transfers between devices, body(): lax.psum_scatter(partial_value, ('particle', 'rep'), scatter_dimension=2,...  12.1 us
    reshape x2, local copies, waits for them, and re-layouts, insert_images(): tiled = spectra.reshape(count, 2, TSIDE, tile_size, TSIDE, tile_size)  9.54 us
    unnamed x19, local copies, waits for them, and re-layouts  7.23 us
    reshape x1, local copies, waits for them, and re-layouts, insert_images(): return added.reshape(plane_total, 2, box_size, box_size)  6.74 us
  transfers between devices with their start and end apart: 4, of which 4 were waited for; matrix products, arithmetic and copies ran while one was open for 19% of the time, Pallas kernels for 0%

commit v1 on v0

--- a/solution.py
+++ b/solution.py
@@ -1,8 +1,13 @@
+import functools
 import math
 
 import jax
 import jax.numpy as jnp
+import ml_dtypes
+import numpy as np
 from jax import lax
+from jax.experimental import pallas as pl
+from jax.experimental.pallas import tpu as pltpu
 from jax.sharding import PartitionSpec as P
 
 ZS = 3
@@ -152,7 +157,263 @@
     return raw / correction
 
 
+BOX = 384
+DEVS = 16
+ROWS = BOX // DEVS
+LINES = 8
+XS = BOX // LINES
+FREQS = 7
+MESH = pl.DeviceIdType.MESH
+F32 = jnp.float32
+BF16 = jnp.bfloat16
+
+
+def host_tables():
+    k = np.arange(BOX)
+    theta = 2.0 * np.pi * ((k[:, None] * k[None, :]) % BOX) / BOX
+    cos, sin = np.cos(theta) / math.sqrt(BOX), np.sin(theta) / math.sqrt(BOX)
+    q = np.where(k < BOX // 2, k, k - BOX)
+    weight = np.sinc(q / BOX) ** 2
+    over_x = np.block([[cos, -sin], [sin, cos]])
+    both = np.stack([np.concatenate([cos, sin], 1), np.concatenate([-sin, cos], 1)])
+    over_y = both.reshape(2, DEVS, ROWS, 2 * BOX).transpose(1, 0, 2, 3).reshape(2 * BOX, 2 * BOX)
+    inverse = np.stack([np.concatenate([cos, -sin], 0), np.concatenate([sin, cos], 0)], 1) / weight
+    inverse = inverse.reshape(2 * BOX, 2, LINES, XS).transpose(0, 2, 1, 3).reshape(2 * BOX, LINES, 2 * XS)
+    back_x = np.zeros((2 * BOX, LINES, 128))
+    back_x[:, :, : 2 * XS] = inverse
+    back_y = np.concatenate([cos / weight, sin / weight], 1)
+    place = np.zeros((FREQS, 256, 32))
+    for n in range(FREQS):
+        for side, kz in enumerate((n - 3, 3 - n)):
+            if kz <= 2:
+                slab, plane = divmod(kz + 3, ZS)
+                for t in range(9):
+                    place[n, slab * 128 + plane * 9 + t, side * 9 + t] = 1.0
+    tables = over_x, over_y, back_x.reshape(2 * BOX, LINES * 128), back_y, place
+    return [t.astype(np.float32).astype(ml_dtypes.bfloat16) for t in tables], weight
+
+
+def device_number():
+    return lax.axis_index("particle") * 4 + lax.axis_index("slab") * 2 + lax.axis_index("rep")
+
+
+def scale_kernel(counts_ref, out_ref):
+    me = device_number()
+    ky = lax.broadcasted_iota(jnp.int32, (ROWS, 128), 0) + me * ROWS
+    ky = jnp.where(ky < BOX // 2, ky, ky - BOX)
+    root = lax.rsqrt(counts_ref[...].astype(F32))
+    for tile in range(3):
+        kx = lax.broadcasted_iota(jnp.int32, (ROWS, 128), 1) + tile * 128
+        kx = jnp.where(kx < BOX // 2, kx, kx - BOX)
+        for kz in range(4):
+            r2 = ky * ky + kx * kx + kz * kz
+            s = jnp.sqrt(r2.astype(F32)).astype(jnp.int32)
+            s = s - (s * s > r2).astype(jnp.int32)
+            s = s + ((s + 1) * (s + 1) <= r2).astype(jnp.int32)
+            low = s % 128
+            total = jnp.zeros((ROWS, 128), F32)
+            for part in range(3):
+                line = jnp.broadcast_to(root[part : part + 1, :], (ROWS, 128))
+                got = jnp.take_along_axis(line, low, axis=1, mode="promise_in_bounds")
+                total = jnp.where(s // 128 == part, got, total)
+            out_ref[kz * ROWS : (kz + 1) * ROWS, tile * 128 : (tile + 1) * 128] = total
+
+
+def main_kernel(
+    weight,
+    img_ref, hot_ref, tab_ref, scale_ref, w1_ref, w2_ref, w3_ref, w4_ref, place_ref,
+    out_ref,
+    hots, tabs, hbuf, gbuf, rbuf, gf, coef, qf, zbuf, zrecv,
+    hot_send, hot_recv, tab_send, tab_recv, g_send, g_recv, z_send, z_recv,
+):
+    me = device_number()
+    group = lax.axis_index("groups")
+    my_slab = lax.axis_index("slab")
+
+    def where_is(d):
+        return (group, d // 4, (d // 2) % 2, d % 2)
+
+    def peer(n):
+        return (me + n) % DEVS
+
+    barrier = pltpu.get_barrier_semaphore()
+    for n in range(1, DEVS):
+        pl.semaphore_signal(barrier, inc=1, device_id=where_is(peer(n)), device_id_type=MESH)
+
+    hots[me] = hot_ref[...]
+    tabs[my_slab] = tab_ref[...]
+    pair = jnp.concatenate([img_ref[0].astype(BF16), img_ref[1].astype(BF16)], axis=1)
+    first = jnp.dot(pair, w1_ref[...], preferred_element_type=F32).astype(BF16)
+    hbuf[0:BOX, :] = first[:, :BOX]
+    hbuf[BOX:, :] = first[:, BOX:]
+
+    pl.semaphore_wait(barrier, DEVS - 1)
+
+    def hot_copy(slot, d):
+        return pltpu.make_async_remote_copy(
+            src_ref=hot_ref, dst_ref=hots.at[slot], send_sem=hot_send.at[d], recv_sem=hot_recv.at[slot],
+            device_id=where_is(d), device_id_type=MESH)
+
+    def tab_copy(slot):
+        return pltpu.make_async_remote_copy(
+            src_ref=tab_ref, dst_ref=tabs.at[slot], send_sem=tab_send, recv_sem=tab_recv,
+            device_id=where_is(me + 2 - 4 * my_slab), device_id_type=MESH)
+
+    def g_copy(slot, d):
+        return pltpu.make_async_remote_copy(
+            src_ref=gbuf.at[d], dst_ref=rbuf.at[slot], send_sem=g_send.at[d], recv_sem=g_recv.at[slot],
+            device_id=where_is(d), device_id_type=MESH)
+
+    def z_copy(slot, d):
+        return pltpu.make_async_remote_copy(
+            src_ref=zbuf.at[d], dst_ref=zrecv.at[slot], send_sem=z_send.at[d], recv_sem=z_recv.at[slot],
+            device_id=where_is(d), device_id_type=MESH)
+
+    tab_copy(my_slab).start()
+    for n in range(1, DEVS):
+        hot_copy(me, peer(n)).start()
+
+    my_quad = me // 4
+    my_place = me % 4
+    for step in (2, 1, 3, 0):
+        quad = (my_quad + step) % 4
+        rows = w2_ref[pl.ds(pl.multiple_of(quad * 192, 192), 192), :]
+        made = jnp.dot(rows, hbuf[...], preferred_element_type=F32).astype(BF16)
+        gbuf[pl.ds(quad * 4, 4)] = made.reshape(4, 2 * ROWS, BOX)
+        for n in range(4 if step else 3):
+            d = quad * 4 + (n if step else (my_place + 1 + n) % 4)
+            g_copy(me, d).start()
+    rbuf[me] = gbuf[me]
+
+    tab_copy(1 - my_slab).wait()
+    for n in range(1, DEVS):
+        hot_copy(peer(n), peer(n)).wait()
+    hot = jnp.concatenate([hots[:, 0, :], hots[:, 1, :]], axis=0)[:, :32].astype(BF16)
+    chosen = jnp.concatenate(
+        [jnp.dot(hot, tabs[s], preferred_element_type=F32).astype(BF16) for s in range(2)], axis=1)
+    mixed = jnp.concatenate(
+        [jnp.dot(chosen, place_ref[n], preferred_element_type=F32).astype(BF16) for n in range(FREQS)], axis=0)
+    lane = lax.broadcasted_iota(jnp.int32, (32, BOX), 1)
+    entry = lax.broadcasted_iota(jnp.int32, (32, BOX), 0)
+    tile = lane // 128
+    mirror = jnp.where(lane == 0, 0, (BOX - lane) // 128)
+    for ch in range(3):
+        for v in range(2):
+            ky = me * ROWS + ch * 8 + (1 - v)
+            at = ky // 128 * 3 + tile
+            mirror_at = 9 + (BOX - ky) % BOX // 128 * 3 + mirror
+            select = ((entry == at) | (entry == mirror_at)).astype(F32).astype(BF16)
+            coef[ch, v] = jnp.dot(mixed, select, preferred_element_type=F32)
+
+    for n in range(1, DEVS):
+        g_copy(peer(n), peer(n)).wait()
+    gf[...] = rbuf[...].astype(F32)
+
+    row_zero = lax.broadcasted_iota(jnp.int32, (8, BOX), 0) == 0
+
+    def per_group(ch, _):
+        base = pl.multiple_of(ch * 8, 8)
+
+        def per_pair(p, sums):
+            gr = gf[p, pl.ds(base, 8), :]
+            gi = gf[p, pl.ds(base + ROWS, 8), :]
+            new = []
+            for n in range(FREQS):
+                one = jnp.where(row_zero, coef[ch, 1, pl.ds(n * 32 + p, 1), :], coef[ch, 0, pl.ds(n * 32 + p, 1), :])
+                two = jnp.where(
+                    row_zero, coef[ch, 1, pl.ds(n * 32 + 16 + p, 1), :], coef[ch, 0, pl.ds(n * 32 + 16 + p, 1), :])
+                new.append(sums[2 * n] + (one * gr + two * gi))
+                new.append(sums[2 * n + 1] + (one * gi - two * gr))
+            return tuple(new)
+
+        sums = lax.fori_loop(0, DEVS, per_pair, tuple(jnp.zeros((8, BOX), F32) for _ in range(2 * FREQS)))
+        scales = [scale_ref[pl.ds(base + ROWS * j, 8), :] for j in range(4)]
+        re = [sums[2 * n] * scales[abs(n - 3)] for n in range(FREQS)]
+        im = [sums[2 * n + 1] * scales[abs(n - 3)] for n in range(FREQS)]
+        even = [(re[3 + j] + re[3 - j], im[3 + j] + im[3 - j]) for j in range(1, 4)]
+        odd = [(re[3 + j] - re[3 - j], im[3 + j] - im[3 - j]) for j in range(1, 4)]
+        for o in range(8):
+            factor = 0.5 / math.sqrt(6.0) / float(weight[o * 48])
+            out_re, out_im = re[3] * factor, im[3] * factor
+            for j in range(1, 4):
+                c = factor * math.cos(2.0 * math.pi * (j * o % 8) / 8)
+                s = factor * math.sin(2.0 * math.pi * (j * o % 8) / 8)
+                out_re = out_re + (c * even[j - 1][0] - s * odd[j - 1][1])
+                out_im = out_im + (c * even[j - 1][1] + s * odd[j - 1][0])
+            qf[pl.ds(base + o * ROWS, 8), 0:BOX] = out_re
+            qf[pl.ds(base + o * ROWS, 8), BOX:] = out_im
+        return 0
+
+    lax.fori_loop(0, 3, per_group, 0)
+
+    for s in range(2):
+        part = qf[s * 96 : (s + 1) * 96, :].astype(BF16)
+        lines = jnp.dot(part, w3_ref[...], preferred_element_type=F32).astype(BF16)
+        for q in range(LINES):
+            zbuf[q // 2 * 4 + s * 2 + q % 2] = lines[:, q * 128 : (q + 1) * 128]
+    for n in (8, 7, 9, 6, 10, 5, 11, 4, 12, 3, 13, 2, 14, 1, 15):
+        z_copy(me, peer(n)).start()
+    zrecv[me] = zbuf[me]
+    for n in range(1, DEVS):
+        z_copy(peer(n), peer(n)).wait()
+    got = zrecv[...].astype(F32)
+    for o in range(4):
+        column = got[:, o * ROWS : (o + 1) * ROWS, :].reshape(BOX, 128).astype(BF16)
+        res = lax.dot_general(column, w4_ref[...], (((0,), (0,)), ((), ())), preferred_element_type=F32)
+        out_ref[o] = res[0:XS, :BOX] - res[XS : 2 * XS, BOX:]
+
+
+def fused(images, poses, plane_index, plane_weight, shell_counts):
+    tables, weight = host_tables()
+    vmem = pl.BlockSpec(memory_space=pltpu.VMEM)
+    counts = jnp.pad(shell_counts, (0, BOX - shell_counts.shape[0]), constant_values=1).reshape(3, 128)
+    scale = pl.pallas_call(
+        scale_kernel,
+        out_shape=jax.ShapeDtypeStruct((4 * ROWS, BOX), F32),
+        in_specs=[vmem],
+        out_specs=vmem,
+        name="shell_scale",
+    )(counts)
+    hot = (poses[:, None] == jnp.arange(128, dtype=jnp.int32)[None, :]).astype(F32)
+    hot = jnp.pad(hot, ((0, 6), (0, 0)))
+    index, entries = plane_index[:, 0], plane_weight[:, 0]
+    planes = jnp.arange(ZS, dtype=jnp.int32)[None, :, None, None]
+    table = jnp.sum(jnp.where(index[:, None] == planes, entries[:, None], 0.0), axis=2)
+    table = jnp.pad(table.reshape(32, 27).astype(BF16), ((0, 0), (0, 101)))
+    return pl.pallas_call(
+        functools.partial(main_kernel, weight),
+        out_shape=jax.ShapeDtypeStruct((4, XS, BOX), F32),
+        in_specs=[vmem] * 9,
+        out_specs=vmem,
+        scratch_shapes=[
+            pltpu.VMEM((DEVS, 8, 128), F32),
+            pltpu.VMEM((2, 32, 128), BF16),
+            pltpu.VMEM((2 * BOX, BOX), BF16),
+            pltpu.VMEM((DEVS, 2 * ROWS, BOX), BF16),
+            pltpu.VMEM((DEVS, 2 * ROWS, BOX), BF16),
+            pltpu.VMEM((DEVS, 2 * ROWS, BOX), F32),
+            pltpu.VMEM((3, 2, FREQS * 32, BOX), F32),
+            pltpu.VMEM((8 * ROWS, 2 * BOX), F32),
+            pltpu.VMEM((DEVS, 96, 128), BF16),
+            pltpu.VMEM((DEVS, 96, 128), BF16),
+            pltpu.SemaphoreType.DMA((DEVS,)),
+            pltpu.SemaphoreType.DMA((DEVS,)),
+            pltpu.SemaphoreType.DMA,
+            pltpu.SemaphoreType.DMA,
+            pltpu.SemaphoreType.DMA((DEVS,)),
+            pltpu.SemaphoreType.DMA((DEVS,)),
+            pltpu.SemaphoreType.DMA((DEVS,)),
+            pltpu.SemaphoreType.DMA((DEVS,)),
+        ],
+        compiler_params=pltpu.CompilerParams(
+            collective_id=0, has_side_effects=True, vmem_limit_bytes=48 * 2**20
+        ),
+        name="reconstruct",
+    )(images, hot, table, scale, *[jnp.asarray(t) for t in tables])
+
+
 def solution(mesh):
+    small = (mesh.shape["particle"], mesh.shape["slab"], mesh.shape["rep"]) == (4, 2, 2)
     in_specs = (
         P(("groups", "particle", "slab", "rep"), None, None),
         P(("groups", "particle", "slab", "rep")),
@@ -161,4 +422,4 @@
         P("groups"),
     )
     out_specs = P(("groups", "slab"), ("particle", "rep"), None)
-    return jax.shard_map(body, mesh=mesh, in_specs=in_specs, out_specs=out_specs, check_vma=False)
+    return jax.shard_map(fused if small else body, mesh=mesh, in_specs=in_specs, out_specs=out_specs, check_vma=False)

time: 177 us -> 49.2 us (0.28)
  waiting for transfers between devices: 52.3 us -> 0 us
  matrix products: 41.8 us -> 0 us
  Pallas kernels: 0 us -> 38.3 us
  local copies, waits for them, and re-layouts: 37.7 us -> 8.89 us
  other arithmetic: 17.5 us -> 1.52 us
  between operations: 14 us -> 0.02 us
  blocking collectives: 5.19 us -> 0 us
  loops' own time: 4.03 us -> 0 us
  starting transfers between devices: 3.8 us -> 0 us
    dot_general x18 -> x0, matrix products: 41.8 us -> none  [the longest x3 19.7 us: plane_scale(): return jnp.dot(member, inverse_root, precision=highest)]
    pallas_call x0 -> x2, Pallas kernels: none -> 38.3 us  [the longest x1 36.6 us: fused(): pl.pallas_call(functools.partial(main_kernel, weight), out_shape=jax.Shap...]
    reduce_scatter x2 -> x0, waiting for transfers between devices: 26.2 us -> none  [the longest x1 14.1 us: body(): lax.psum_scatter(jnp.einsum('zo,zxy->oxy', depth_cos, pencil_lines[:, 0],...]
    reshape x3 -> x1, local copies, waits for them, and re-layouts: 16.3 us -> 1.25 us  [fused(): jnp.pad(shell_counts, (0, BOX - shell_counts.shape[0]), constant_values=1)]
    all_to_all x1 -> x0, waiting for transfers between devices: 13.2 us -> none  [body(): lax.all_to_all(across, ('particle', 'rep'), split_axis=2, concat_axis=3,...]
    all_gather x1 -> x0, waiting for transfers between devices: 12.8 us -> none  [body(): lax.all_gather(images.astype(jnp.bfloat16), 'slab', axis=0, tiled=True)]
    transpose x2 -> x0, local copies, waits for them, and re-layouts: 6.91 us -> none  [the longest x1 4.55 us: insert_images(): jnp.einsum('zabi,icaybx->zcaybx', mixing, tiled, preferred_element_type=j...]
    unnamed x1 -> x0, blocking collectives: 5.19 us -> none
  transfers between devices with their start and end apart: 4 -> 0, of which waited for: 4 -> 0; matrix products, arithmetic and copies ran while one was open for 19% -> 0% of each run, Pallas kernels for 0% -> 0%
where the time goes in v1:
time: 49.2 us; the launch traced here: 48.8 us
  Pallas kernels  38.3 us (78%)
  local copies, waits for them, and re-layouts  8.89 us (18%)
  other arithmetic  1.52 us (3%)
    pallas_call x1, Pallas kernels, fused(): pl.pallas_call(functools.partial(main_kernel, weight), out_shape=jax.Shap...  36.6 us
    unnamed x13, local copies, waits for them, and re-layouts  7.52 us
    pallas_call x1, Pallas kernels, fused(): pl.pallas_call(scale_kernel, out_shape=jax.ShapeDtypeStruct((4 * ROWS, BO...  1.71 us
    reshape x1, local copies, waits for them, and re-layouts, fused(): jnp.pad(shell_counts, (0, BOX - shell_counts.shape[0]), constant_values=1)  1.25 us

profile of v1, /device:TPU:0, one launch (start us, length us, event | category | flops | bytes accessed | tf_op | source)
XLA Modules:
  0.0 48.8 jit_solution(17068353259320030433)
XLA Ops:
  0.0 0.7 %iota_compare_fusion.1 = pred[2,128]{1,0:T(4,128)(4,1)S(1)} fusion(s32[2]{0:T(128)} %param.11), kind=kLoop, calls=%fused_computation.4 | loop fusion | flops 256 | bytes 264 | tf_op jit(solution)/shard_map/eq | solution.py:377
  0.7 1.2 %pad_bitcast_fusion.counts_ref = s32[3,128]{1,0:T(4,128)} fusion(s32[288]{0:T(512)} %param.14), kind=kLoop, calls=%fused_computation.3 | loop fusion | bytes 2688 | tf_op jit(solution)/shard_map/reshape | solution.py:369
  2.0 0.8 %select_reduce_fusion = bf16[32,3,9]{0,2,1:T(8,128)(2,1)S(1)} fusion(f32[32,4,9]{0,1,2:T(4,128)} %bitcast.6, s32[32,4,9]{0,1,2:T(4,128)} %bitcast.7), kind=kLoop, calls=%fused_computation | loop fusion | flops 9504 | bytes 10944 | tf_op jit(solution)/shard_map/reduce_sum | solution.py:381
  2.8 0.1 copy.16
  2.9 1.7 %shell_scale.1.scale_ref = f32[96,384]{1,0:T(8,128)} custom-call(s32[3,128]{1,0:T(4,128)} %pad_bitcast_fusion.counts_ref), custom_call_target="tpu_custom_call" | custom-call | tf_op jit(solution)/shard_map/shell_scale/pallas_call | solution.py:370
  4.6 0.0 copy-start
  4.6 1.3 %copy-done = f32[2,384,384]{2,1,0:T(8,128)S(1)} copy-done((f32[2,384,384]{2,1,0:T(8,128)S(1)}, f32[2,384,384]{2,1,0:T(8,128)}, u32[]{:S(2)}) %copy-start) | copy-done | bytes 1179672
  5.9 0.0 copy-start.1
  5.9 1.3 %copy-done.1 = bf16[768,768]{1,0:T(8,128)(2,1)S(1)} copy-done((bf16[768,768]{1,0:T(8,128)(2,1)S(1)}, bf16[768,768]{1,0:T(8,128)(2,1)}, u32[]{:S(2)}) %copy-start.1) | copy-done | bytes 1179672
  7.2 0.0 copy-start.2
  7.2 1.3 %copy-done.2 = bf16[768,768]{1,0:T(8,128)(2,1)S(1)} copy-done((bf16[768,768]{1,0:T(8,128)(2,1)S(1)}, bf16[768,768]{1,0:T(8,128)(2,1)}, u32[]{:S(2)}) %copy-start.2) | copy-done | bytes 1179672
  8.4 0.0 copy-start.3
  8.4 0.9 %copy-done.3 = f32[96,384]{1,0:T(8,128)S(1)} copy-done((f32[96,384]{1,0:T(8,128)S(1)}, f32[96,384]{1,0:T(8,128)}, u32[]{:S(2)}) %copy-start.3) | copy-done | bytes 147480
  9.3 0.0 copy-start.4
  9.3 1.1 %copy-done.4 = bf16[384,768]{1,0:T(8,128)(2,1)S(1)} copy-done((bf16[384,768]{1,0:T(8,128)(2,1)S(1)}, bf16[384,768]{1,0:T(8,128)(2,1)}, u32[]{:S(2)}) %copy-start.4) | copy-done | bytes 589848
  10.4 0.0 copy-start.5
  10.4 1.0 %copy-done.5 = bf16[7,256,32]{2,1,0:T(8,128)(2,1)S(1)} copy-done((bf16[7,256,32]{2,1,0:T(8,128)(2,1)S(1)}, bf16[7,256,32]{2,1,0:T(8,128)(2,1)}, u32[]{:S(2)}) %copy-start.5) | copy-done | bytes 114712
  11.4 36.6 %reconstruct.1 = f32[4,48,384]{2,1,0:T(8,128)S(1)} custom-call(f32[2,384,384]{2,1,0:T(8,128)S(1)} %copy-done, f32[8,128]{1,0:T(8,128)S(1)} %pad_convert_fusion.hot_ref, bf16[32,128]{1,0:T(8,128)(2,1)S(1)} %pad.16.tab_ref, f32[96,384]{1,0:T(8,128)S(1)} %copy-done.3, bf16[768,768]{1,0:T(8,128)(2,1)S(1)} %copy-done.2, bf16[768,768]{1,0:T(8,128)(2,1)S(1)} %copy-done.1, ...), custom_call_target="tpu_custom_call" | custom-call | tf_op jit(solution)/shard_map/reconstruct/pallas_call | solution.py:383
  48.1 0.7 %copy.18 = f32[4,48,384]{2,1,0:T(8,128)} copy(f32[4,48,384]{2,1,0:T(8,128)S(1)} %reconstruct.1) | data formatting | bytes 589824
  (3 shorter events, 0.0 us)
Async XLA Ops:
  4.6 1.3 %copy-start = (f32[2,384,384]{2,1,0:T(8,128)S(1)}, f32[2,384,384]{2,1,0:T(8,128)}, u32[]{:S(2)}) copy-start(f32[2,384,384]{2,1,0:T(8,128)} %img_ref.1) | copy-start | bytes 3538948
  5.9 1.3 %copy-start.1 = (bf16[768,768]{1,0:T(8,128)(2,1)S(1)}, bf16[768,768]{1,0:T(8,128)(2,1)}, u32[]{:S(2)}) copy-start(bf16[768,768]{1,0:T(8,128)(2,1)} %constant.21.clone.w2_ref) | copy-start | bytes 3538948
  7.2 1.3 %copy-start.2 = (bf16[768,768]{1,0:T(8,128)(2,1)S(1)}, bf16[768,768]{1,0:T(8,128)(2,1)}, u32[]{:S(2)}) copy-start(bf16[768,768]{1,0:T(8,128)(2,1)} %constant.20.clone.w1_ref) | copy-start | bytes 3538948
  8.4 0.9 %copy-start.3 = (f32[96,384]{1,0:T(8,128)S(1)}, f32[96,384]{1,0:T(8,128)}, u32[]{:S(2)}) copy-start(f32[96,384]{1,0:T(8,128)} %shell_scale.1.scale_ref) | copy-start | bytes 442372
  9.3 1.1 %copy-start.4 = (bf16[384,768]{1,0:T(8,128)(2,1)S(1)}, bf16[384,768]{1,0:T(8,128)(2,1)}, u32[]{:S(2)}) copy-start(bf16[384,768]{1,0:T(8,128)(2,1)} %constant.23.clone.w4_ref) | copy-start | bytes 1769476
  10.4 1.0 %copy-start.5 = (bf16[7,256,32]{2,1,0:T(8,128)(2,1)S(1)}, bf16[7,256,32]{2,1,0:T(8,128)(2,1)}, u32[]{:S(2)}) copy-start(bf16[7,256,32]{2,1,0:T(8,128)(2,1)} %constant.24.clone.place_ref) | copy-start | bytes 344068

commit v2 on v1

--- a/solution.py
+++ b/solution.py
@@ -168,6 +168,14 @@
 BF16 = jnp.bfloat16
 
 
+def ky_of(me, row):
+    back = row >= 12
+    j = row - 4 * (back & (row < 16)) - 16 * (row >= 16)
+    slot = me * 12 + j
+    ky = slot + ((slot >= 128) & (slot < 132)) - 4 * (slot == 132)
+    return ky + back * (BOX - 2 * ky - (BOX // 2) * (slot == 0))
+
+
 def host_tables():
     k = np.arange(BOX)
     theta = 2.0 * np.pi * ((k[:, None] * k[None, :]) % BOX) / BOX
@@ -176,12 +184,23 @@
     weight = np.sinc(q / BOX) ** 2
     over_x = np.block([[cos, -sin], [sin, cos]])
     both = np.stack([np.concatenate([cos, sin], 1), np.concatenate([-sin, cos], 1)])
-    over_y = both.reshape(2, DEVS, ROWS, 2 * BOX).transpose(1, 0, 2, 3).reshape(2 * BOX, 2 * BOX)
-    inverse = np.stack([np.concatenate([cos, -sin], 0), np.concatenate([sin, cos], 0)], 1) / weight
-    inverse = inverse.reshape(2 * BOX, 2, LINES, XS).transpose(0, 2, 1, 3).reshape(2 * BOX, LINES, 2 * XS)
-    back_x = np.zeros((2 * BOX, LINES, 128))
-    back_x[:, :, : 2 * XS] = inverse
-    back_y = np.concatenate([cos / weight, sin / weight], 1)
+    order = ky_of(np.arange(DEVS)[:, None], np.arange(ROWS)[None, :])
+    over_y = both[:, order].transpose(1, 0, 2, 3).reshape(2 * BOX, 2 * BOX)
+    def lines(table):
+        padded = np.zeros((2 * BOX, LINES, 64))
+        padded[:, :, :XS] = (table / weight).reshape(2 * BOX, LINES, XS)
+        return padded.reshape(2 * BOX, LINES * 64)
+
+    back_x = np.stack([lines(np.concatenate([cos, -sin], 0)), lines(np.concatenate([sin, cos], 0))])
+    positive = order[:, :12]
+    parts = [cos[positive] / weight, sin[positive] / weight]
+    parts[1][0, 0] = -cos[BOX // 2] / weight
+    basis = np.concatenate(parts, 2)
+    back_y = np.zeros((2, 2, DEVS, 8, 2 * BOX))
+    for parity in range(2):
+        back_y[parity, 0] = basis[:, :8]
+        back_y[parity, 1, :, 4 * parity : 4 * parity + 4] = basis[:, 8:]
+    back_y = back_y.reshape(2, 2 * DEVS * 8, 2 * BOX)
     place = np.zeros((FREQS, 256, 32))
     for n in range(FREQS):
         for side, kz in enumerate((n - 3, 3 - n)):
@@ -189,7 +208,7 @@
                 slab, plane = divmod(kz + 3, ZS)
                 for t in range(9):
                     place[n, slab * 128 + plane * 9 + t, side * 9 + t] = 1.0
-    tables = over_x, over_y, back_x.reshape(2 * BOX, LINES * 128), back_y, place
+    tables = over_x, over_y, back_x, back_y, place
     return [t.astype(np.float32).astype(ml_dtypes.bfloat16) for t in tables], weight
 
 
@@ -199,9 +218,13 @@
 
 def scale_kernel(counts_ref, out_ref):
     me = device_number()
-    ky = lax.broadcasted_iota(jnp.int32, (ROWS, 128), 0) + me * ROWS
-    ky = jnp.where(ky < BOX // 2, ky, ky - BOX)
-    root = lax.rsqrt(counts_ref[...].astype(F32))
+    row = lax.broadcasted_iota(jnp.int32, (ROWS, 128), 0)
+    back = row >= 12
+    slot = me * 12 + jnp.where(back, jnp.where(row < 16, row - 4, row - 16), row)
+    ky = jnp.where((slot >= 128) & (slot < 132), slot + 1, jnp.where(slot == 132, 128, slot))
+    ky = jnp.where(back & (slot == 0), BOX // 2, ky)
+    filled = jnp.concatenate([counts_ref[...], jnp.ones((1, BOX - counts_ref.shape[1]), jnp.int32)], axis=1)
+    root = lax.rsqrt(filled.astype(F32))
     for tile in range(3):
         kx = lax.broadcasted_iota(jnp.int32, (ROWS, 128), 1) + tile * 128
         kx = jnp.where(kx < BOX // 2, kx, kx - BOX)
@@ -213,7 +236,7 @@
             low = s % 128
             total = jnp.zeros((ROWS, 128), F32)
             for part in range(3):
-                line = jnp.broadcast_to(root[part : part + 1, :], (ROWS, 128))
+                line = jnp.broadcast_to(root[:, part * 128 : (part + 1) * 128], (ROWS, 128))
                 got = jnp.take_along_axis(line, low, axis=1, mode="promise_in_bounds")
                 total = jnp.where(s // 128 == part, got, total)
             out_ref[kz * ROWS : (kz + 1) * ROWS, tile * 128 : (tile + 1) * 128] = total
@@ -221,10 +244,11 @@
 
 def main_kernel(
     weight,
-    img_ref, hot_ref, tab_ref, scale_ref, w1_ref, w2_ref, w3_ref, w4_ref, place_ref,
+    img_hbm, poses_ref, index_ref, entry_ref, scale_ref, w1_hbm, w2_hbm, w3_hbm, w4_hbm, place_hbm,
     out_ref,
+    img_ref, w1_ref, w2_ref, w3_ref, w4_ref, place_ref, hot_ref, tab_ref,
     hots, tabs, hbuf, gbuf, rbuf, gf, coef, qf, zbuf, zrecv,
-    hot_send, hot_recv, tab_send, tab_recv, g_send, g_recv, z_send, z_recv,
+    hot_send, hot_recv, tab_send, tab_recv, g_send, g_recv, z_send, z_recv, load_sem,
 ):
     me = device_number()
     group = lax.axis_index("groups")
@@ -240,8 +264,29 @@
     for n in range(1, DEVS):
         pl.semaphore_signal(barrier, inc=1, device_id=where_is(peer(n)), device_id_type=MESH)
 
+    loads = [
+        pltpu.make_async_copy(src, dst, load_sem.at[n])
+        for n, (src, dst) in enumerate([
+            (img_hbm, img_ref), (w1_hbm, w1_ref), (w2_hbm, w2_ref), (place_hbm, place_ref),
+            (w3_hbm, w3_ref), (w4_hbm, w4_ref)])
+    ]
+    for load in loads:
+        load.start()
+
+    spot = lax.broadcasted_iota(jnp.int32, (8, 128), 1)
+    line = lax.broadcasted_iota(jnp.int32, (8, 128), 0)
+    hot_ref[...] = (spot == jnp.where(line == 0, poses_ref[0], poses_ref[1])).astype(F32)
+    planes = []
+    for z in range(ZS):
+        total = jnp.zeros((32, 9), F32)
+        for e in range(4):
+            total = total + jnp.where(index_ref[e] == z, entry_ref[e], 0.0)
+        planes.append(total)
+    tab_ref[...] = jnp.concatenate(planes + [jnp.zeros((32, 101), F32)], axis=1).astype(BF16)
     hots[me] = hot_ref[...]
     tabs[my_slab] = tab_ref[...]
+    loads[0].wait()
+    loads[1].wait()
     pair = jnp.concatenate([img_ref[0].astype(BF16), img_ref[1].astype(BF16)], axis=1)
     first = jnp.dot(pair, w1_ref[...], preferred_element_type=F32).astype(BF16)
     hbuf[0:BOX, :] = first[:, :BOX]
@@ -273,6 +318,7 @@
     for n in range(1, DEVS):
         hot_copy(me, peer(n)).start()
 
+    loads[2].wait()
     my_quad = me // 4
     my_place = me % 4
     for step in (2, 1, 3, 0):
@@ -285,6 +331,7 @@
             g_copy(me, d).start()
     rbuf[me] = gbuf[me]
 
+    loads[3].wait()
     tab_copy(1 - my_slab).wait()
     for n in range(1, DEVS):
         hot_copy(peer(n), peer(n)).wait()
@@ -299,7 +346,7 @@
     mirror = jnp.where(lane == 0, 0, (BOX - lane) // 128)
     for ch in range(3):
         for v in range(2):
-            ky = me * ROWS + ch * 8 + (1 - v)
+            ky = ky_of(me, ch * 8 + (4 * v if ch == 1 else 1 - v))
             at = ky // 128 * 3 + tile
             mirror_at = 9 + (BOX - ky) % BOX // 128 * 3 + mirror
             select = ((entry == at) | (entry == mirror_at)).astype(F32).astype(BF16)
@@ -309,10 +356,11 @@
         g_copy(peer(n), peer(n)).wait()
     gf[...] = rbuf[...].astype(F32)
 
-    row_zero = lax.broadcasted_iota(jnp.int32, (8, BOX), 0) == 0
+    sub = lax.broadcasted_iota(jnp.int32, (8, BOX), 0)
 
     def per_group(ch, _):
         base = pl.multiple_of(ch * 8, 8)
+        row_zero = jnp.where(ch == 1, 7 - sub, sub) < jnp.where(ch == 1, 4, 1)
 
         def per_pair(p, sums):
             gr = gf[p, pl.ds(base, 8), :]
@@ -340,52 +388,77 @@
                 s = factor * math.sin(2.0 * math.pi * (j * o % 8) / 8)
                 out_re = out_re + (c * even[j - 1][0] - s * odd[j - 1][1])
                 out_im = out_im + (c * even[j - 1][1] + s * odd[j - 1][0])
-            qf[pl.ds(base + o * ROWS, 8), 0:BOX] = out_re
-            qf[pl.ds(base + o * ROWS, 8), BOX:] = out_im
+            qf[ch, o, :, 0:BOX] = out_re
+            qf[ch, o, :, BOX:] = out_im
         return 0
 
     lax.fori_loop(0, 3, per_group, 0)
 
+    loads[4].wait()
+    wide = lax.broadcasted_iota(jnp.int32, (8, 2 * BOX), 0)
+    own = (wide == 0) & (me == 0)
+    sums, diffs = [], []
     for s in range(2):
-        part = qf[s * 96 : (s + 1) * 96, :].astype(BF16)
-        lines = jnp.dot(part, w3_ref[...], preferred_element_type=F32).astype(BF16)
-        for q in range(LINES):
-            zbuf[q // 2 * 4 + s * 2 + q % 2] = lines[:, q * 128 : (q + 1) * 128]
+        for o in range(4 * s, 4 * s + 4):
+            a, c = qf[0, o], qf[2, o]
+            turned = jnp.concatenate([-c[:, BOX:], c[:, :BOX]], axis=1)
+            sums.append(jnp.where(own, a, a + c))
+            diffs.append(jnp.where(own, turned, a - c))
+        for o in (4 * s, 4 * s + 2):
+            a, b = qf[1, o], qf[1, o + 1]
+            ra, rb = pltpu.roll(a, 4, axis=0), pltpu.roll(b, 4, axis=0)
+            sums.append(jnp.where(wide < 4, a + ra, b + rb))
+            diffs.append(jnp.where(wide < 4, a - ra, rb - b))
+    real = jnp.dot(jnp.concatenate(sums, axis=0).astype(BF16), w3_ref[0], preferred_element_type=F32)
+    imag = jnp.dot(jnp.concatenate(diffs, axis=0).astype(BF16), w3_ref[1], preferred_element_type=F32)
+    left = lax.broadcasted_iota(jnp.int32, (96, 128), 1) < 64
+    for pair_of in range(4):
+        r = real[:, pair_of * 128 : (pair_of + 1) * 128]
+        i = imag[:, pair_of * 128 : (pair_of + 1) * 128]
+        even_line = jnp.where(left, r, pltpu.roll(i, 64, axis=1)).astype(BF16)
+        odd_line = jnp.where(left, pltpu.roll(r, 64, axis=1), i).astype(BF16)
+        for s in range(2):
+            zbuf[pair_of * 4 + s * 2] = even_line[s * 48 : (s + 1) * 48]
+            zbuf[pair_of * 4 + s * 2 + 1] = odd_line[s * 48 : (s + 1) * 48]
     for n in (8, 7, 9, 6, 10, 5, 11, 4, 12, 3, 13, 2, 14, 1, 15):
         z_copy(me, peer(n)).start()
     zrecv[me] = zbuf[me]
+    loads[5].wait()
     for n in range(1, DEVS):
         z_copy(peer(n), peer(n)).wait()
     got = zrecv[...].astype(F32)
     for o in range(4):
-        column = got[:, o * ROWS : (o + 1) * ROWS, :].reshape(BOX, 128).astype(BF16)
-        res = lax.dot_general(column, w4_ref[...], (((0,), (0,)), ((), ())), preferred_element_type=F32)
-        out_ref[o] = res[0:XS, :BOX] - res[XS : 2 * XS, BOX:]
+        shared = 32 + o // 2 * 8
+        column = jnp.concatenate(
+            [got[:, o * 8 : o * 8 + 8, :].reshape(128, 128), got[:, shared : shared + 8, :].reshape(128, 128)],
+            axis=0).astype(BF16)
+        res = lax.dot_general(column, w4_ref[o % 2], (((0,), (0,)), ((), ())), preferred_element_type=F32)
+        out_ref[o] = res[0:XS, :BOX] - res[64 : 64 + XS, BOX:]
 
 
 def fused(images, poses, plane_index, plane_weight, shell_counts):
     tables, weight = host_tables()
     vmem = pl.BlockSpec(memory_space=pltpu.VMEM)
-    counts = jnp.pad(shell_counts, (0, BOX - shell_counts.shape[0]), constant_values=1).reshape(3, 128)
     scale = pl.pallas_call(
         scale_kernel,
         out_shape=jax.ShapeDtypeStruct((4 * ROWS, BOX), F32),
         in_specs=[vmem],
         out_specs=vmem,
         name="shell_scale",
-    )(counts)
-    hot = (poses[:, None] == jnp.arange(128, dtype=jnp.int32)[None, :]).astype(F32)
-    hot = jnp.pad(hot, ((0, 6), (0, 0)))
-    index, entries = plane_index[:, 0], plane_weight[:, 0]
-    planes = jnp.arange(ZS, dtype=jnp.int32)[None, :, None, None]
-    table = jnp.sum(jnp.where(index[:, None] == planes, entries[:, None], 0.0), axis=2)
-    table = jnp.pad(table.reshape(32, 27).astype(BF16), ((0, 0), (0, 101)))
+    )(shell_counts.reshape(1, -1))
+    whole = pl.BlockSpec(memory_space=pl.ANY)
+    index = plane_index[:, 0].transpose(1, 0, 2)
+    entries = plane_weight[:, 0].transpose(1, 0, 2)
     return pl.pallas_call(
         functools.partial(main_kernel, weight),
         out_shape=jax.ShapeDtypeStruct((4, XS, BOX), F32),
-        in_specs=[vmem] * 9,
+        in_specs=[whole, pl.BlockSpec(memory_space=pltpu.SMEM), vmem, vmem, vmem] + [whole] * 5,
         out_specs=vmem,
         scratch_shapes=[
+            pltpu.VMEM(images.shape, F32),
+            *[pltpu.VMEM(t.shape, BF16) for t in tables],
+            pltpu.VMEM((8, 128), F32),
+            pltpu.VMEM((32, 128), BF16),
             pltpu.VMEM((DEVS, 8, 128), F32),
             pltpu.VMEM((2, 32, 128), BF16),
             pltpu.VMEM((2 * BOX, BOX), BF16),
@@ -393,9 +466,9 @@
             pltpu.VMEM((DEVS, 2 * ROWS, BOX), BF16),
             pltpu.VMEM((DEVS, 2 * ROWS, BOX), F32),
             pltpu.VMEM((3, 2, FREQS * 32, BOX), F32),
-            pltpu.VMEM((8 * ROWS, 2 * BOX), F32),
-            pltpu.VMEM((DEVS, 96, 128), BF16),
-            pltpu.VMEM((DEVS, 96, 128), BF16),
+            pltpu.VMEM((3, 8, 8, 2 * BOX), F32),
+            pltpu.VMEM((DEVS, 48, 128), BF16),
+            pltpu.VMEM((DEVS, 48, 128), BF16),
             pltpu.SemaphoreType.DMA((DEVS,)),
             pltpu.SemaphoreType.DMA((DEVS,)),
             pltpu.SemaphoreType.DMA,
@@ -404,12 +477,13 @@
             pltpu.SemaphoreType.DMA((DEVS,)),
             pltpu.SemaphoreType.DMA((DEVS,)),
             pltpu.SemaphoreType.DMA((DEVS,)),
+            pltpu.SemaphoreType.DMA((6,)),
         ],
         compiler_params=pltpu.CompilerParams(
             collective_id=0, has_side_effects=True, vmem_limit_bytes=48 * 2**20
         ),
         name="reconstruct",
-    )(images, hot, table, scale, *[jnp.asarray(t) for t in tables])
+    )(images, poses, index, entries, scale, *[jnp.asarray(t) for t in tables])
 
 
 def solution(mesh):

time: 49.2 us -> 45.5 us (0.925)
  Pallas kernels: 38.3 us -> 33.8 us
  local copies, waits for them, and re-layouts: 8.89 us -> 11.1 us
  other arithmetic: 1.52 us -> 0 us
    pallas_call x1, Pallas kernels: 36.6 us -> 32.1 us  [fused(): pl.pallas_call(functools.partial(main_kernel, weight), out_shape=jax.Shap...]
    unnamed x13 -> x17, local copies, waits for them, and re-layouts: 7.52 us -> 9.88 us
    reduce_sum x1 -> x0, other arithmetic: 0.79 us -> none  [fused(): jnp.sum(jnp.where(index[:, None] == planes, entries[:, None], 0.0), axis=2)]
    eq x1 -> x0, other arithmetic: 0.73 us -> none  [fused(): poses[:, None] == jnp.arange(128, dtype=jnp.int32)[None, :]]
where the time goes in v2:
time: 45.5 us; the launch traced here: 45 us
  Pallas kernels  33.8 us (74%)
  local copies, waits for them, and re-layouts  11.1 us (24%)
    pallas_call x1, Pallas kernels, fused(): pl.pallas_call(functools.partial(main_kernel, weight), out_shape=jax.Shap...  32.1 us
    unnamed x17, local copies, waits for them, and re-layouts  9.88 us
    pallas_call x1, Pallas kernels, fused(): pl.pallas_call(scale_kernel, out_shape=jax.ShapeDtypeStruct((4 * ROWS, BO...  1.71 us
    reshape x1, local copies, waits for them, and re-layouts, fused(): shell_counts.reshape(1, -1)  1.27 us

profile of v2, /device:TPU:0, one launch (start us, length us, event | category | flops | bytes accessed | tf_op | source)
XLA Modules:
  0.0 45.0 jit_solution(17738230992589689502)
XLA Ops:
  0.0 1.3 %reshape.3.counts_ref = s32[1,288]{1,0:T(1,128)} reshape(s32[288]{0:T(512)} %param.14) | data formatting | bytes 2304 | tf_op jit(solution)/shard_map/reshape | solution.py:448
  1.3 0.8 %copy.11 = s32[32,1,4,9]{3,0,2,1:T(8,128)S(1)} copy(s32[32,1,4,9]{0,2,3,1:T(4,128)} %param.12) | data formatting | bytes 9216 | tf_op args[2]
  2.1 0.8 %copy.12 = f32[32,1,4,9]{3,0,2,1:T(8,128)S(1)} copy(f32[32,1,4,9]{0,2,3,1:T(4,128)} %param.13) | data formatting | bytes 9216 | tf_op args[3]
  2.9 1.7 %shell_scale.1.scale_ref = f32[96,384]{1,0:T(8,128)} custom-call(s32[1,288]{1,0:T(1,128)} %reshape.3.counts_ref), custom_call_target="tpu_custom_call" | custom-call | tf_op jit(solution)/shard_map/shell_scale/pallas_call | solution.py:442
  4.6 0.0 copy-start
  4.6 1.3 %copy-done = f32[2,384,384]{2,1,0:T(8,128)S(1)} copy-done((f32[2,384,384]{2,1,0:T(8,128)S(1)}, f32[2,384,384]{2,1,0:T(8,128)}, u32[]{:S(2)}) %copy-start) | copy-done | bytes 1179672
  5.9 0.0 copy-start.1
  5.9 1.3 %copy-done.1 = bf16[768,768]{1,0:T(8,128)(2,1)S(1)} copy-done((bf16[768,768]{1,0:T(8,128)(2,1)S(1)}, bf16[768,768]{1,0:T(8,128)(2,1)}, u32[]{:S(2)}) %copy-start.1) | copy-done | bytes 1179672
  7.2 0.0 copy-start.2
  7.2 1.3 %copy-done.2 = bf16[768,768]{1,0:T(8,128)(2,1)S(1)} copy-done((bf16[768,768]{1,0:T(8,128)(2,1)S(1)}, bf16[768,768]{1,0:T(8,128)(2,1)}, u32[]{:S(2)}) %copy-start.2) | copy-done | bytes 1179672
  8.4 0.0 copy-start.3
  8.4 1.1 %copy-done.3 = bf16[2,256,768]{2,1,0:T(8,128)(2,1)S(1)} copy-done((bf16[2,256,768]{2,1,0:T(8,128)(2,1)S(1)}, bf16[2,256,768]{2,1,0:T(8,128)(2,1)}, u32[]{:S(2)}) %copy-start.3) | copy-done | bytes 786456
  9.6 0.0 copy-start.4
  9.6 0.9 %copy-done.4 = f32[96,384]{1,0:T(8,128)S(1)} copy-done((f32[96,384]{1,0:T(8,128)S(1)}, f32[96,384]{1,0:T(8,128)}, u32[]{:S(2)}) %copy-start.4) | copy-done | bytes 147480
  10.5 0.0 copy-start.5
  10.5 1.0 %copy-done.5 = bf16[7,256,32]{2,1,0:T(8,128)(2,1)S(1)} copy-done((bf16[7,256,32]{2,1,0:T(8,128)(2,1)S(1)}, bf16[7,256,32]{2,1,0:T(8,128)(2,1)}, u32[]{:S(2)}) %copy-start.5) | copy-done | bytes 114712
  11.5 0.0 copy-start.6
  11.5 0.7 %copy-done.6 = s32[2]{0:T(128)S(1)} copy-done((s32[2]{0:T(128)S(1)}, s32[2]{0:T(128)}, u32[]{:S(2)}) %copy-start.6) | copy-done | bytes 32
  12.2 32.1 %reconstruct.1 = f32[4,48,384]{2,1,0:T(8,128)S(1)} custom-call(f32[2,384,384]{2,1,0:T(8,128)S(1)} %copy-done, s32[2]{0:T(128)S(1)} %copy-done.6, s32[4,32,9]{2,1,0:T(8,128)S(1)} %bitcast.6, f32[4,32,9]{2,1,0:T(8,128)S(1)} %bitcast.7, f32[96,384]{1,0:T(8,128)S(1)} %copy-done.4, bf16[768,768]{1,0:T(8,128)(2,1)S(1)} %copy-done.2, ...), custom_call_target="tpu_custom_call" | custom-call | tf_op jit(solution)/shard_map/reconstruct/pallas_call | solution.py:452
  44.3 0.7 %copy.14 = f32[4,48,384]{2,1,0:T(8,128)} copy(f32[4,48,384]{2,1,0:T(8,128)S(1)} %reconstruct.1) | data formatting | bytes 589824
Async XLA Ops:
  4.6 1.3 %copy-start = (f32[2,384,384]{2,1,0:T(8,128)S(1)}, f32[2,384,384]{2,1,0:T(8,128)}, u32[]{:S(2)}) copy-start(f32[2,384,384]{2,1,0:T(8,128)} %img_hbm.1) | copy-start | bytes 3538948
  5.9 1.3 %copy-start.1 = (bf16[768,768]{1,0:T(8,128)(2,1)S(1)}, bf16[768,768]{1,0:T(8,128)(2,1)}, u32[]{:S(2)}) copy-start(bf16[768,768]{1,0:T(8,128)(2,1)} %constant.11.clone.w2_hbm) | copy-start | bytes 3538948
  7.2 1.3 %copy-start.2 = (bf16[768,768]{1,0:T(8,128)(2,1)S(1)}, bf16[768,768]{1,0:T(8,128)(2,1)}, u32[]{:S(2)}) copy-start(bf16[768,768]{1,0:T(8,128)(2,1)} %constant.10.clone.w1_hbm) | copy-start | bytes 3538948
  8.4 1.1 %copy-start.3 = (bf16[2,256,768]{2,1,0:T(8,128)(2,1)S(1)}, bf16[2,256,768]{2,1,0:T(8,128)(2,1)}, u32[]{:S(2)}) copy-start(bf16[2,256,768]{2,1,0:T(8,128)(2,1)} %constant.13.clone.w4_hbm) | copy-start | bytes 2359300
  9.6 0.9 %copy-start.4 = (f32[96,384]{1,0:T(8,128)S(1)}, f32[96,384]{1,0:T(8,128)}, u32[]{:S(2)}) copy-start(f32[96,384]{1,0:T(8,128)} %shell_scale.1.scale_ref) | copy-start | bytes 442372
  10.5 1.0 %copy-start.5 = (bf16[7,256,32]{2,1,0:T(8,128)(2,1)S(1)}, bf16[7,256,32]{2,1,0:T(8,128)(2,1)}, u32[]{:S(2)}) copy-start(bf16[7,256,32]{2,1,0:T(8,128)(2,1)} %constant.14.clone.place_hbm) | copy-start | bytes 344068
  11.5 0.7 %copy-start.6 = (s32[2]{0:T(128)S(1)}, s32[2]{0:T(128)}, u32[]{:S(2)}) copy-start(s32[2]{0:T(128)} %poses_ref.1) | copy-start | bytes 28

commit v3 on v2

--- a/solution.py
+++ b/solution.py
@@ -201,13 +201,13 @@
         back_y[parity, 0] = basis[:, :8]
         back_y[parity, 1, :, 4 * parity : 4 * parity + 4] = basis[:, 8:]
     back_y = back_y.reshape(2, 2 * DEVS * 8, 2 * BOX)
-    place = np.zeros((FREQS, 256, 32))
+    place = np.zeros((FREQS, 64, 32))
     for n in range(FREQS):
         for side, kz in enumerate((n - 3, 3 - n)):
             if kz <= 2:
                 slab, plane = divmod(kz + 3, ZS)
                 for t in range(9):
-                    place[n, slab * 128 + plane * 9 + t, side * 9 + t] = 1.0
+                    place[n, slab * 32 + plane * 9 + t, side * 9 + t] = 1.0
     tables = over_x, over_y, back_x, back_y, place
     return [t.astype(np.float32).astype(ml_dtypes.bfloat16) for t in tables], weight
 
@@ -216,14 +216,14 @@
     return lax.axis_index("particle") * 4 + lax.axis_index("slab") * 2 + lax.axis_index("rep")
 
 
-def scale_kernel(counts_ref, out_ref):
+def shell_scales(counts_ref, out_ref):
     me = device_number()
     row = lax.broadcasted_iota(jnp.int32, (ROWS, 128), 0)
     back = row >= 12
     slot = me * 12 + jnp.where(back, jnp.where(row < 16, row - 4, row - 16), row)
     ky = jnp.where((slot >= 128) & (slot < 132), slot + 1, jnp.where(slot == 132, 128, slot))
     ky = jnp.where(back & (slot == 0), BOX // 2, ky)
-    filled = jnp.concatenate([counts_ref[...], jnp.ones((1, BOX - counts_ref.shape[1]), jnp.int32)], axis=1)
+    filled = jnp.concatenate([counts_ref[...].reshape(1, -1), jnp.ones((1, BOX - counts_ref.shape[0]), jnp.int32)], axis=1)
     root = lax.rsqrt(filled.astype(F32))
     for tile in range(3):
         kx = lax.broadcasted_iota(jnp.int32, (ROWS, 128), 1) + tile * 128
@@ -242,11 +242,15 @@
             out_ref[kz * ROWS : (kz + 1) * ROWS, tile * 128 : (tile + 1) * 128] = total
 
 
+def _nt(left, right):
+    return lax.dot_general(left, right, (((1,), (1,)), ((), ())), preferred_element_type=F32)
+
+
 def main_kernel(
     weight,
-    img_hbm, poses_ref, index_ref, entry_ref, scale_ref, w1_hbm, w2_hbm, w3_hbm, w4_hbm, place_hbm,
+    img_hbm, poses_ref, index_ref, entry_ref, counts_ref, w1_hbm, w2_hbm, w3_hbm, w4_hbm, place_hbm,
     out_ref,
-    img_ref, w1_ref, w2_ref, w3_ref, w4_ref, place_ref, hot_ref, tab_ref,
+    img_ref, w1_ref, w2_ref, w3_ref, w4_ref, place_ref, hot_ref, tab_ref, scale_ref, acc,
     hots, tabs, hbuf, gbuf, rbuf, gf, coef, qf, zbuf, zrecv,
     hot_send, hot_recv, tab_send, tab_recv, g_send, g_recv, z_send, z_recv, load_sem,
 ):
@@ -278,11 +282,8 @@
     hot_ref[...] = (spot == jnp.where(line == 0, poses_ref[0], poses_ref[1])).astype(F32)
     planes = []
     for z in range(ZS):
-        total = jnp.zeros((32, 9), F32)
-        for e in range(4):
-            total = total + jnp.where(index_ref[e] == z, entry_ref[e], 0.0)
-        planes.append(total)
-    tab_ref[...] = jnp.concatenate(planes + [jnp.zeros((32, 101), F32)], axis=1).astype(BF16)
+        planes.append(jnp.sum(jnp.where(index_ref[...] == z, entry_ref[...], 0.0), axis=1))
+    tab_ref[...] = jnp.concatenate(planes + [jnp.zeros((5, 32), F32)], axis=0).astype(BF16)
     hots[me] = hot_ref[...]
     tabs[my_slab] = tab_ref[...]
     loads[0].wait()
@@ -321,15 +322,18 @@
     loads[2].wait()
     my_quad = me // 4
     my_place = me % 4
-    for step in (2, 1, 3, 0):
-        quad = (my_quad + step) % 4
+    half, side = my_quad // 2, my_quad % 2
+    quads = (2 - 2 * half + side, 3 - 2 * half - side, 2 * half + 1 - side, my_quad)
+    for quad in quads:
         rows = w2_ref[pl.ds(pl.multiple_of(quad * 192, 192), 192), :]
         made = jnp.dot(rows, hbuf[...], preferred_element_type=F32).astype(BF16)
         gbuf[pl.ds(quad * 4, 4)] = made.reshape(4, 2 * ROWS, BOX)
-        for n in range(4 if step else 3):
-            d = quad * 4 + (n if step else (my_place + 1 + n) % 4)
+        for n in range(3 if quad is my_quad else 4):
+            d = quad * 4 + ((my_place + 1 + n) % 4 if quad is my_quad else n)
             g_copy(me, d).start()
     rbuf[me] = gbuf[me]
+
+    shell_scales(counts_ref, scale_ref)
 
     loads[3].wait()
     tab_copy(1 - my_slab).wait()
@@ -337,7 +341,7 @@
         hot_copy(peer(n), peer(n)).wait()
     hot = jnp.concatenate([hots[:, 0, :], hots[:, 1, :]], axis=0)[:, :32].astype(BF16)
     chosen = jnp.concatenate(
-        [jnp.dot(hot, tabs[s], preferred_element_type=F32).astype(BF16) for s in range(2)], axis=1)
+        [_nt(hot, tabs[s]).astype(BF16) for s in range(2)], axis=1)
     mixed = jnp.concatenate(
         [jnp.dot(chosen, place_ref[n], preferred_element_type=F32).astype(BF16) for n in range(FREQS)], axis=0)
     lane = lax.broadcasted_iota(jnp.int32, (32, BOX), 1)
@@ -352,29 +356,44 @@
             select = ((entry == at) | (entry == mirror_at)).astype(F32).astype(BF16)
             coef[ch, v] = jnp.dot(mixed, select, preferred_element_type=F32)
 
-    for n in range(1, DEVS):
-        g_copy(peer(n), peer(n)).wait()
-    gf[...] = rbuf[...].astype(F32)
-
     sub = lax.broadcasted_iota(jnp.int32, (8, BOX), 0)
+
+    acc[...] = jnp.zeros(acc.shape, F32)
+    for quad in (quads[3], quads[2], quads[0], quads[1]):
+        for n in range(3 if quad is my_quad else 4):
+            d = quad * 4 + ((my_place + 1 + n) % 4 if quad is my_quad else n)
+            g_copy(d, d).wait()
+        gf[...] = rbuf[pl.ds(quad * 4, 4)].astype(F32)
+
+        def add_group(ch, _):
+            base = pl.multiple_of(ch * 8, 8)
+            row_zero = jnp.where(ch == 1, 7 - sub, sub) < jnp.where(ch == 1, 4, 1)
+
+            def per_pair(i, sums):
+                p = quad * 4 + i
+                gr = gf[i, pl.ds(base, 8), :]
+                gi = gf[i, pl.ds(base + ROWS, 8), :]
+                new = []
+                for n in range(FREQS):
+                    one = jnp.where(
+                        row_zero, coef[ch, 1, pl.ds(n * 32 + p, 1), :], coef[ch, 0, pl.ds(n * 32 + p, 1), :])
+                    two = jnp.where(
+                        row_zero, coef[ch, 1, pl.ds(n * 32 + 16 + p, 1), :],
+                        coef[ch, 0, pl.ds(n * 32 + 16 + p, 1), :])
+                    new.append(sums[2 * n] + (one * gr + two * gi))
+                    new.append(sums[2 * n + 1] + (one * gi - two * gr))
+                return tuple(new)
+
+            sums = lax.fori_loop(0, 4, per_pair, tuple(acc[ch, n] for n in range(2 * FREQS)))
+            for n in range(2 * FREQS):
+                acc[ch, n] = sums[n]
+            return 0
+
+        lax.fori_loop(0, 3, add_group, 0)
 
     def per_group(ch, _):
         base = pl.multiple_of(ch * 8, 8)
-        row_zero = jnp.where(ch == 1, 7 - sub, sub) < jnp.where(ch == 1, 4, 1)
-
-        def per_pair(p, sums):
-            gr = gf[p, pl.ds(base, 8), :]
-            gi = gf[p, pl.ds(base + ROWS, 8), :]
-            new = []
-            for n in range(FREQS):
-                one = jnp.where(row_zero, coef[ch, 1, pl.ds(n * 32 + p, 1), :], coef[ch, 0, pl.ds(n * 32 + p, 1), :])
-                two = jnp.where(
-                    row_zero, coef[ch, 1, pl.ds(n * 32 + 16 + p, 1), :], coef[ch, 0, pl.ds(n * 32 + 16 + p, 1), :])
-                new.append(sums[2 * n] + (one * gr + two * gi))
-                new.append(sums[2 * n + 1] + (one * gi - two * gr))
-            return tuple(new)
-
-        sums = lax.fori_loop(0, DEVS, per_pair, tuple(jnp.zeros((8, BOX), F32) for _ in range(2 * FREQS)))
+        sums = [acc[ch, n] for n in range(2 * FREQS)]
         scales = [scale_ref[pl.ds(base + ROWS * j, 8), :] for j in range(4)]
         re = [sums[2 * n] * scales[abs(n - 3)] for n in range(FREQS)]
         im = [sums[2 * n + 1] * scales[abs(n - 3)] for n in range(FREQS)]
@@ -439,16 +458,9 @@
 def fused(images, poses, plane_index, plane_weight, shell_counts):
     tables, weight = host_tables()
     vmem = pl.BlockSpec(memory_space=pltpu.VMEM)
-    scale = pl.pallas_call(
-        scale_kernel,
-        out_shape=jax.ShapeDtypeStruct((4 * ROWS, BOX), F32),
-        in_specs=[vmem],
-        out_specs=vmem,
-        name="shell_scale",
-    )(shell_counts.reshape(1, -1))
-    whole = pl.BlockSpec(memory_space=pl.ANY)
-    index = plane_index[:, 0].transpose(1, 0, 2)
-    entries = plane_weight[:, 0].transpose(1, 0, 2)
+    whole = pl.BlockSpec(memory_space=pltpu.HBM)
+    index = plane_index[:, 0].transpose(2, 1, 0)
+    entries = plane_weight[:, 0].transpose(2, 1, 0)
     return pl.pallas_call(
         functools.partial(main_kernel, weight),
         out_shape=jax.ShapeDtypeStruct((4, XS, BOX), F32),
@@ -458,13 +470,15 @@
             pltpu.VMEM(images.shape, F32),
             *[pltpu.VMEM(t.shape, BF16) for t in tables],
             pltpu.VMEM((8, 128), F32),
-            pltpu.VMEM((32, 128), BF16),
+            pltpu.VMEM((32, 32), BF16),
+            pltpu.VMEM((4 * ROWS, BOX), F32),
+            pltpu.VMEM((3, 2 * FREQS, 8, BOX), F32),
             pltpu.VMEM((DEVS, 8, 128), F32),
-            pltpu.VMEM((2, 32, 128), BF16),
+            pltpu.VMEM((2, 32, 32), BF16),
             pltpu.VMEM((2 * BOX, BOX), BF16),
             pltpu.VMEM((DEVS, 2 * ROWS, BOX), BF16),
             pltpu.VMEM((DEVS, 2 * ROWS, BOX), BF16),
-            pltpu.VMEM((DEVS, 2 * ROWS, BOX), F32),
+            pltpu.VMEM((4, 2 * ROWS, BOX), F32),
             pltpu.VMEM((3, 2, FREQS * 32, BOX), F32),
             pltpu.VMEM((3, 8, 8, 2 * BOX), F32),
             pltpu.VMEM((DEVS, 48, 128), BF16),
@@ -480,10 +494,10 @@
             pltpu.SemaphoreType.DMA((6,)),
         ],
         compiler_params=pltpu.CompilerParams(
-            collective_id=0, has_side_effects=True, vmem_limit_bytes=48 * 2**20
+            collective_id=0, has_side_effects=True, vmem_limit_bytes=56 * 2**20
         ),
         name="reconstruct",
-    )(images, poses, index, entries, scale, *[jnp.asarray(t) for t in tables])
+    )(images, poses, index, entries, shell_counts, *[jnp.asarray(t) for t in tables])
 
 
 def solution(mesh):

time: 45.5 us -> 33.6 us (0.74)
  local copies, waits for them, and re-layouts: 11.1 us -> 1.69 us
  Pallas kernels: 33.8 us -> 31.7 us
    unnamed x17 -> x1, local copies, waits for them, and re-layouts: 9.88 us -> 1.69 us
    pallas_call x1 -> x0, Pallas kernels: 1.71 us -> none  [fused(): pl.pallas_call(scale_kernel, out_shape=jax.ShapeDtypeStruct((4 * ROWS, BO...]
    reshape x1 -> x0, local copies, waits for them, and re-layouts: 1.27 us -> none  [fused(): shell_counts.reshape(1, -1)]
where the time goes in v3:
time: 33.6 us; the launch traced here: 33.4 us
  Pallas kernels  31.7 us (94%)
  local copies, waits for them, and re-layouts  1.69 us (5%)
    pallas_call x1, Pallas kernels, fused(): pl.pallas_call(functools.partial(main_kernel, weight), out_shape=jax.Shap...  31.7 us
    unnamed x1, local copies, waits for them, and re-layouts  1.69 us

profile of v3, /device:TPU:0, one launch (start us, length us, event | category | flops | bytes accessed | tf_op | source)
XLA Modules:
  0.0 33.4 jit_solution(210424610248478004)
XLA Ops:
  0.0 31.7 %reconstruct.1 = f32[4,48,384]{2,1,0:T(8,128)} custom-call(f32[2,384,384]{2,1,0:T(8,128)} %img_hbm.1, s32[2]{0:T(128)} %poses_ref.1, s32[9,4,32]{2,1,0:T(4,128)} %bitcast.6, f32[9,4,32]{2,1,0:T(4,128)} %bitcast.7, s32[288]{0:T(512)} %counts_ref.1, bf16[768,768]{1,0:T(8,128)(2,1)} %constant.10.clone.w1_hbm, bf16[768,768]{1,0:T(8,128)(2,1)} %constant.11.clone.w2_hbm, ...), custom_call_target="tpu_custom_call" | custom-call | tf_op jit(solution)/shard_map/reconstruct/pallas_call | solution.py:464
  31.7 1.7 %copy.12 = f32[4,48,384]{2,1,0:T(8,128)} copy(f32[4,48,384]{2,1,0:T(8,128)} %reconstruct.1) | data formatting | bytes 589824
